TPU v7x, 512 devices: a whole 4x8x8 slice. The times are simulated.
512 devices in a mesh: row: 16 (over z, y_lo), col: 32 (over x, y_hi, core).
Axes of the slice: x: 4, y: 8 (y_hi: 4, y_lo: 2; y = y_hi * 2 + y_lo), z: 8, core: 2. Of those that a mesh axis runs over, the one named last changes fastest.
Arguments:
- ratings: bfloat16 [16, 96, 512, 512], P('row', 'col'), may hold values from 0 to 3, as said below
- tile_items: int32 [16, 96], P('row', 'col'), may hold values from 0 to 3, as said below
- tile_live: int32 [16, 96], P('row', 'col'), may hold values from 0 to 1, as said below
- item_factors: float32 [65536, 256], P(('col', 'row'))
Outputs:
- user_factors: float32 [8192, 256], P(('row', 'col'))
Inputs may be any that keep to these rules, and one draw needn't show every extreme that they name: `tile_items`: on each device the 3 slots name distinct item blocks. `tile_live`: the first slot of each device (every third entry of the second dimension, starting at 0) is live. `ratings`: entries are zero or positive.
All inputs are finite; a program needn't handle non-finite values.
Results may differ from a plain program's by a relative error of at most 0.0003.
Values sent between devices are 32-bit elements; how exact they have to be, the bound alone decides.
A program may use at most 64 MiB of HBM per device.

v0:
```python
import jax
import jax.numpy as jnp
from jax import lax
from jax.sharding import PartitionSpec as P

ITERS = 3


CONFIDENCE_SCALE = 40.0
RIDGE = 1.0
DIVISOR_GUARD = 1e-20
HIGH = lax.Precision.HIGHEST


def rated_weights(tile_block, live_flag, preference):
    rating = tile_block.astype(jnp.float32)
    if preference:
        weight = jnp.where(rating > 0.0, 1.0 + CONFIDENCE_SCALE * rating, 0.0)
    else:
        weight = CONFIDENCE_SCALE * rating
    return weight * live_flag.astype(jnp.float32)


def tile_term(tile_block, live_flag, item_rows, vectors):
    if vectors is None:
        inner_part = rated_weights(tile_block, live_flag, True)
    else:
        scores = lax.dot_general(
            vectors,
            item_rows,
            (((1,), (1,)), ((), ())),
            precision=HIGH,
            preferred_element_type=jnp.float32,
        )
        inner_part = rated_weights(tile_block, live_flag, False) * scores
    return jnp.dot(inner_part, item_rows, precision=HIGH, preferred_element_type=jnp.float32)


def local_partial(ratings, tile_items, tile_live, local_items, vectors):
    side = ratings.shape[2]
    width = local_items.shape[1]
    running = jnp.zeros((side, width), jnp.float32)
    for slot_index in range(ratings.shape[1]):
        offset = tile_items[0, slot_index] * side
        item_rows = lax.dynamic_slice_in_dim(local_items, offset, side, 0)
        tile_block = ratings[0, slot_index]
        live_flag = tile_live[0, slot_index]
        tile_sum = tile_term(tile_block, live_flag, item_rows, vectors)
        running = running + tile_sum
    return running


def per_device(ratings, tile_items, tile_live, item_factors):
    local_items = lax.all_gather(item_factors, "row", axis=0, tiled=True)
    gram_local = lax.dot_general(
        item_factors,
        item_factors,
        (((0,), (0,)), ((), ())),
        precision=HIGH,
        preferred_element_type=jnp.float32,
    )
    gram_matrix = lax.psum(gram_local, ("row", "col"))

    def confidence(vectors):
        return local_partial(ratings, tile_items, tile_live, local_items, vectors)

    def combine(partial_rows):
        return lax.psum_scatter(partial_rows, "col", scatter_dimension=0, tiled=True)

    rhs = combine(confidence(None))
    solution = jnp.zeros_like(rhs)
    residual = rhs
    direction = rhs
    norm_now = jnp.sum(residual * residual, axis=1, keepdims=True)
    for iteration in range(ITERS):
        product_rows = (
            jnp.dot(direction, gram_matrix, precision=HIGH, preferred_element_type=jnp.float32)
            + RIDGE * direction
            + combine(confidence(lax.all_gather(direction, "col", axis=0, tiled=True)))
        )
        curvature = jnp.sum(direction * product_rows, axis=1, keepdims=True)
        step_size = norm_now / (curvature + DIVISOR_GUARD)
        solution = solution + step_size * direction
        residual = residual - step_size * product_rows
        norm_next = jnp.sum(residual * residual, axis=1, keepdims=True)
        direction = residual + norm_next / (norm_now + DIVISOR_GUARD) * direction
        norm_now = norm_next
    return solution


def solution(mesh):
    placed = (
        P("row", "col", None, None),
        P("row", "col"),
        P("row", "col"),
        P(("col", "row"), None),
    )
    return jax.shard_map(
        per_device, mesh=mesh, in_specs=placed, out_specs=P(("row", "col"), None), check_vma=False
    )
```

profile of v0, /device:TPU:1, one launch (start us, length us, event | category | flops | bytes accessed | tf_op | source)
XLA Modules:
  0.0 670.2 jit_solution(10076726903569662587)
XLA Ops:
  7.4 0.0 all-gather.2.cloned.1.call-start
  7.4 0.7 all-gather.2.cloned.1.call-update
  8.1 0.0 reduce-scatter.5.cloned.1.call-start
  8.1 1.4 fusion.93
  11.4 1.4 fusion.94
  14.7 70.8 %all-gather.2.cloned.1.call-done = f32[2048,256]{1,0:T(8,128)} async-done(((f32[128,256]{1,0:T(8,128)}), f32[2048,256]{1,0:T(8,128)}) %all-gather.2.cloned.1.call-update) | async-done | bytes 2097168 | tf_op jit(solution)/shard_map/all_gather | solution.py:54
  85.5 0.0 copy-start
  85.5 2.5 fusion.9
  88.0 0.0 copy-done
  88.0 2.2 convolution_add_fusion.7
  90.2 0.0 copy-start.5
  90.2 3.0 convolution_add_fusion.6
  93.2 0.0 reduce-scatter.5.cloned.1.call-update
  93.2 0.0 all-reduce.2.cloned.1.call-start
  93.3 0.0 copy-done.5
  93.3 1.1 fusion.95
  94.4 0.0 all-reduce.2.cloned.1.call-update
  94.5 0.0 reduce-scatter.7.cloned.1.call-start
  94.5 102.2 %reduce-scatter.5.cloned.1.call-done = f32[16,256]{1,0:T(8,128)} async-done(((f32[512,256]{1,0:T(8,128)}), f32[16,256]{1,0:T(8,128)}) %reduce-scatter.5.cloned.1.call-update) | async-done | bytes 16400 | tf_op jit(solution)/shard_map/reduce_scatter | solution.py:68
  196.8 46.7 %all_gather.13 = f32[512,256]{1,0:T(8,128)S(1)} all-gather(f32[16,256]{1,0:T(8,128)} %reduce-scatter.5.cloned.1.call-done), channel_id=1, replica_groups=mesh['row'=16,'col'=32] {'col'}, dimensions={0}, use_global_device_ids=true | all-gather | bytes 540672 | tf_op jit(solution)/shard_map/all_gather | solution.py:79
  243.5 0.0 copy-start.1
  243.5 2.2 convolution_multiply_fusion.8
  245.7 1.0 fusion.59
  246.7 0.0 copy-done.1
  246.7 1.1 convolution_multiply_fusion.7
  247.8 1.1 convolution_multiply_fusion.6
  248.8 1.0 convolution_add_fusion.5
  249.8 0.0 copy-start.6
  249.9 1.8 convolution_add_fusion.4
  251.6 0.0 reduce-scatter.7.cloned.1.call-update
  251.7 0.0 reduce-scatter.9.cloned.1.call-start
  251.7 123.1 %all-reduce.2.cloned.1.call-done = f32[256,256]{1,0:T(8,128)} async-done(((f32[256,256]{1,0:T(8,128)}), f32[256,256]{1,0:T(8,128)}) %all-reduce.2.cloned.1.call-update) | async-done | bytes 262160 | tf_op jit(solution)/shard_map/psum | solution.py:62
  374.8 0.0 copy-done.6
  374.8 1.4 multiply_reduce_fusion.3
  376.2 0.2 multiply_reduce_fusion.2
  376.4 0.1 multiply_add_fusion.2
  376.5 44.0 %all_gather.14 = f32[512,256]{1,0:T(8,128)S(1)} all-gather(f32[16,256]{1,0:T(8,128)S(1)} %multiply_add_fusion.2), channel_id=1, replica_groups=mesh['row'=16,'col'=32] {'col'}, dimensions={0}, use_global_device_ids=true | all-gather | bytes 540672 | tf_op jit(solution)/shard_map/all_gather | solution.py:79
  420.5 2.1 convolution_multiply_fusion.5
  422.6 0.0 copy-done.2
  422.6 1.1 convolution_multiply_fusion.4
  423.7 1.1 convolution_multiply_fusion.3
  424.8 1.0 fusion.56
  425.8 1.0 convolution_add_fusion.3
  426.8 0.0 copy-start.4
  426.8 1.8 convolution_add_fusion.2
  428.6 0.0 reduce-scatter.9.cloned.1.call-update
  428.6 0.0 reduce-scatter.11.cloned.1.call-start
  428.7 88.2 %reduce-scatter.9.cloned.1.call-done = f32[16,256]{1,0:T(8,128)} async-done(((f32[512,256]{1,0:T(8,128)}), f32[16,256]{1,0:T(8,128)}) %reduce-scatter.9.cloned.1.call-update) | async-done | bytes 16400 | tf_op jit(solution)/shard_map/reduce_scatter | solution.py:68
  516.9 0.0 copy-done.4
  516.9 1.2 multiply_reduce_fusion.1
  518.1 0.2 multiply_reduce_fusion
  518.3 0.1 multiply_add_fusion.1
  518.4 46.7 %all_gather.15 = f32[512,256]{1,0:T(8,128)S(1)} all-gather(f32[16,256]{1,0:T(8,128)S(1)} %multiply_add_fusion.1), channel_id=1, replica_groups=mesh['row'=16,'col'=32] {'col'}, dimensions={0}, use_global_device_ids=true | all-gather | bytes 540672 | tf_op jit(solution)/shard_map/all_gather | solution.py:79
  565.1 2.1 convolution_multiply_fusion.2
  567.2 0.0 copy-done.3
  567.2 1.1 convolution_multiply_fusion.1
  568.3 1.1 convolution_multiply_fusion
  569.4 1.0 fusion.53
  570.4 1.0 convolution_add_fusion.1
  571.4 1.8 convolution_add_fusion
  573.2 0.0 reduce-scatter.11.cloned.1.call-update
  573.2 88.1 %reduce-scatter.11.cloned.1.call-done = f32[16,256]{1,0:T(8,128)} async-done(((f32[512,256]{1,0:T(8,128)}), f32[16,256]{1,0:T(8,128)}) %reduce-scatter.11.cloned.1.call-update) | async-done | bytes 16400 | tf_op jit(solution)/shard_map/reduce_scatter | solution.py:68
  661.3 1.1 fusion.4
  662.4 0.7 multiply_add_fusion
  (8 shorter events, 0.0 us)
Async XLA Ops:
  7.4 78.1 %all-gather.2.cloned.1.call-start = ((), (), s32[]{:S(2)}) async-start(), calls=%async_computation.4 | async-start | bytes 2228224 | tf_op jit(solution)/shard_map/all_gather | solution.py:54
  8.1 188.7 %reduce-scatter.5.cloned.1.call-start = ((), (), s32[]{:S(2)}) async-start(), calls=%async_computation.5 | async-start | bytes 540672 | tf_op jit(solution)/shard_map/reduce_scatter | solution.py:68
  85.5 2.5 copy-start
  90.2 3.1 copy-start.5
  93.2 281.6 %all-reduce.2.cloned.1.call-start = ((), (), s32[]{:S(2)}) async-start(), calls=%async_computation.6 | async-start | bytes 524288 | tf_op jit(solution)/shard_map/psum | solution.py:62
  94.5 280.4 %reduce-scatter.7.cloned.1.call-start = ((), (), s32[]{:S(2)}) async-start(), calls=%async_computation.7 | async-start | bytes 540672 | tf_op jit(solution)/shard_map/reduce_scatter | solution.py:68
  243.5 3.2 copy-start.1
  249.8 125.0 %copy-start.6 = (f32[16,256]{1,0:T(8,128)S(1)}, f32[16,256]{1,0:T(8,128)}, u32[]{:S(2)}) copy-start(f32[16,256]{1,0:T(8,128)} %reduce-scatter.5.cloned.1.call-done) | copy-start | bytes 49156
  251.7 265.2 %reduce-scatter.9.cloned.1.call-start = ((), (), s32[]{:S(2)}) async-start(), calls=%async_computation.8 | async-start | bytes 540672 | tf_op jit(solution)/shard_map/reduce_scatter | solution.py:68
  374.8 47.8 %copy-start.2 = (bf16[1,3,512,512]{3,2,1,0:T(8,128)(2,1)S(1)}, bf16[1,3,512,512]{3,2,1,0:T(8,128)(2,1)}, u32[]{:S(2)}) copy-start(bf16[1,3,512,512]{3,2,1,0:T(8,128)(2,1)} %param.4) | copy-start | bytes 4718596
  426.8 90.1 %copy-start.4 = (f32[256,256]{1,0:T(8,128)S(1)}, f32[256,256]{1,0:T(8,128)}, u32[]{:S(2)}) copy-start(f32[256,256]{1,0:T(8,128)} %all-reduce.2.cloned.1.call-done) | copy-start | bytes 786436
  428.6 232.7 %reduce-scatter.11.cloned.1.call-start = ((), (), s32[]{:S(2)}) async-start(), calls=%async_computation.9 | async-start | bytes 540672 | tf_op jit(solution)/shard_map/reduce_scatter | solution.py:68
  516.9 50.3 %copy-start.3 = (bf16[1,3,512,512]{3,2,1,0:T(8,128)(2,1)S(1)}, bf16[1,3,512,512]{3,2,1,0:T(8,128)(2,1)}, u32[]{:S(2)}) copy-start(bf16[1,3,512,512]{3,2,1,0:T(8,128)(2,1)} %param.4) | copy-start | bytes 4718596
Sparse Core Ops, SparseCore 0:
  10.3 75.1 all-gather.1
  93.4 103.3 reduce-scatter.4
  251.8 88.2 reduce-scatter.6
  428.7 88.1 reduce-scatter.8
  573.3 87.9 reduce-scatter.10
Sparse Core Ops, SparseCore 1:
  98.7 276.1 all-reduce.1
where the time goes:
time: 671 us; the launch traced here: 670 us
  waiting for transfers between devices  473 us (70%)
  blocking collectives  137 us (20%)
  matrix products  36.6 us (5%)
  between operations  18.6 us (3%)
    reduce_scatter x4, waiting for transfers between devices, combine(): lax.psum_scatter(partial_rows, 'col', scatter_dimension=0, tiled=True)  279 us
    all_gather x3, blocking collectives, per_device(): lax.all_gather(direction, 'col', axis=0, tiled=True)  137 us
    psum x1, waiting for transfers between devices, per_device(): gram_matrix = lax.psum(gram_local, ('row', 'col'))  123 us
    all_gather x1, waiting for transfers between devices, per_device(): local_items = lax.all_gather(item_factors, 'row', axis=0, tiled=True)  70.8 us
    dot_general x12, matrix products, tile_term(): jnp.dot(inner_part, item_rows, precision=HIGH, preferred_element_type=jnp...  19 us
  transfers between devices with their start and end apart: 6, of which 5 were waited for; matrix products, arithmetic and copies ran while one was open for 2% of the time, Pallas kernels for 0%

commit v1 on v0

v1 whole, which is shorter than its diff:
```python
import functools

import jax
import jax.numpy as jnp
from jax import lax
from jax.experimental import pallas as pl
from jax.experimental.pallas import tpu as pltpu
from jax.sharding import PartitionSpec as P

ITERS = 3
CONFIDENCE_SCALE = 40.0
RIDGE = 1.0
DIVISOR_GUARD = 1e-20

K = 256
TB = 512
BLOCKS = 4
SLOTS = 3
Z = 8
CHIPS = 16
STREAMS = 1
OWN = 16 // STREAMS
HALF = CHIPS * OWN
CUT = 56
SHARE = 128
MESH = pl.DeviceIdType.MESH
F32 = jnp.float32
BF16 = jnp.bfloat16

NN = (((1,), (0,)), ((), ()))
NT = (((1,), (1,)), ((), ()))
TN = (((0,), (0,)), ((), ()))


def split(value):
    high = value.astype(BF16)
    return high, (value - high.astype(F32)).astype(BF16)


def dot(a, b, dims):
    return lax.dot_general(a, b, dims, preferred_element_type=F32)


def dot3(a, b, dims):
    return dot(a[0], b[0], dims) + (dot(a[1], b[0], dims) + dot(a[0], b[1], dims))


def kernel(
    tile_ref, live_ref, ratings_ref, items_ref, out_ref,
    items, raw, weights, item_high, item_low, scaled_high, scaled_low, gram_high, gram_low,
    vectors, partial, from_core, summed, from_chips, direction, lane_sums, lane_core, lane_total, lane_chips,
    load_sem, z_send, z_recv, y_send, y_recv, core_send, core_recv, reduce_send, reduce_recv,
    gather_send, gather_recv, back_send, back_recv, last_send, last_recv,
):
    row = lax.axis_index("row")
    col = lax.axis_index("col")
    z, y_lo = row // 2, row % 2
    chip, core = col // 2, col % 2
    other_core = 1 - core

    def chip_at(offset):
        return ((chip // 4 + offset // 4) % 4) * 4 + (chip % 4 + offset % 4) % 4

    def opposite(offset):
        return (-(offset // 4) % 4) * 4 + -(offset % 4) % 4

    to_core = (row, chip * 2 + other_core)
    to_y = (z * 2 + 1 - y_lo, col)
    to_z = {1: (((z + 1) % Z) * 2 + y_lo, col), -1: (((z + Z - 1) % Z) * 2 + y_lo, col)}
    to_chip = {k: (row, chip_at(k) * 2 + core) for k in range(1, CHIPS)}

    pending = []

    def send(src, dst, send_sem, recv_sem, device):
        copy = pltpu.make_async_remote_copy(
            src_ref=src, dst_ref=dst, send_sem=send_sem, recv_sem=recv_sem, device_id=device, device_id_type=MESH
        )
        copy.start()
        pending.append(copy)

    def arrived(dst, send_sem, recv_sem, device):
        pltpu.make_async_remote_copy(
            src_ref=dst, dst_ref=dst, send_sem=send_sem, recv_sem=recv_sem, device_id=device, device_id_type=MESH
        ).wait_recv()

    def item_rows(z_of, y_of, first, count):
        return items.at[pl.ds(pl.multiple_of((z_of * 2 + y_of) * SHARE + first, 8), count)]

    own_load = pltpu.make_async_copy(items_ref, item_rows(z, y_lo, 0, SHARE), load_sem.at[0])
    own_load.start()
    rating_loads = [
        pltpu.make_async_copy(ratings_ref.at[:, :, c], raw.at[:, c], load_sem.at[1 + c]) for c in range(2)
    ]
    for load in rating_loads:
        load.start()

    barrier = pltpu.get_barrier_semaphore()
    neighbours = [to_core, to_y, to_z[1], to_z[-1]] + list(to_chip.values())
    for device in neighbours:
        pl.semaphore_signal(barrier, inc=1, device_id=device, device_id_type=MESH)
    own_load.wait()
    pl.semaphore_wait(barrier, len(neighbours))

    def z_piece(kind, z_of):
        if kind == 0:
            return item_rows(z_of, y_lo, 0, CUT)
        if kind == 1:
            return item_rows(z_of, y_lo, CUT, SHARE - CUT)
        return item_rows(z_of, 1 - y_lo, 0, CUT)

    reach = {(0, 1): 4, (0, -1): 3, (1, 1): 3, (1, -1): 4, (2, 1): 4, (2, -1): 3}

    def z_index(kind, way, hop):
        return (kind * 2 + (way + 1) // 2) * 4 + hop - 1

    def z_source(way, hop):
        return (z + Z - way * hop) % Z

    def z_send_piece(kind, way, hop):
        piece = z_piece(kind, z_source(way, hop - 1))
        index = z_index(kind, way, hop)
        send(piece, piece, z_send.at[index], z_recv.at[index], to_z[way])

    def y_send_piece(index, z_of, first, count):
        piece = item_rows(z_of, y_lo, first, count)
        send(piece, piece, y_send.at[index], y_recv.at[index], to_y)

    y_send_piece(0, z, 0, CUT)
    for kind in (0, 1):
        for way in (1, -1):
            z_send_piece(kind, way, 1)
    y_send_piece(1, z, CUT, SHARE - CUT)
    arrived(item_rows(z, 1 - y_lo, 0, CUT), y_send.at[0], y_recv.at[0], to_y)
    for way in (1, -1):
        z_send_piece(2, way, 1)
    crossing = [(1, z)]
    for hop in range(1, 5):
        for kind in (0, 1, 2):
            for way in (1, -1):
                if hop > reach[kind, way]:
                    continue
                source = z_source(way, hop)
                index = z_index(kind, way, hop)
                arrived(z_piece(kind, source), z_send.at[index], z_recv.at[index], to_z[-way])
                if hop < reach[kind, way]:
                    z_send_piece(kind, way, hop + 1)
                if kind == 1:
                    y_index = len(crossing) + 1
                    y_send_piece(y_index, source, CUT, SHARE - CUT)
                    crossing.append((y_index, source))
    for load in rating_loads:
        load.wait()
    for slot in range(SLOTS):
        for half in range(2):
            block = raw[slot, half].astype(F32)
            for stream in range(STREAMS):
                part = block[:, stream * OWN:(stream + 1) * OWN, :]
                weights[stream, slot, half * HALF:(half + 1) * HALF, :] = part.reshape(HALF, TB)
    for y_index, source in crossing:
        piece = item_rows(source, 1 - y_lo, CUT, SHARE - CUT)
        arrived(piece, y_send.at[y_index], y_recv.at[y_index], to_y)

    live = [live_ref[0, slot].astype(F32) for slot in range(SLOTS)]
    gram_even = jnp.zeros((K, K), F32)
    gram_odd = jnp.zeros((K, K), F32)
    for block in range(BLOCKS):
        high, low = split(items[block * TB:(block + 1) * TB, :])
        gram_even += dot(high, high, TN)
        gram_odd += dot(high, low, TN)
    gram_high[...], gram_low[...] = split(gram_even + (gram_odd + gram_odd.T))
    for slot in range(SLOTS):
        block = jnp.zeros((TB, K), F32)
        for index in range(BLOCKS):
            block += (tile_ref[0, slot] == index).astype(F32) * items[index * TB:(index + 1) * TB, :]
        item_high[slot], item_low[slot] = split(block)
        scaled_high[slot], scaled_low[slot] = split(block * (CONFIDENCE_SCALE * live[slot]))

    def reduce_start(phase, stream):
        send(
            partial.at[phase, stream, other_core], from_core.at[phase, stream],
            core_send.at[phase, stream], core_recv.at[phase, stream], to_core,
        )

    def reduce_middle(phase, stream):
        arrived(from_core.at[phase, stream], core_send.at[phase, stream], core_recv.at[phase, stream], to_core)
        summed[phase, stream] = partial[phase, stream, core] + from_core[phase, stream]
        for k in range(1, CHIPS):
            start = pl.multiple_of(chip_at(k) * OWN, OWN)
            send(
                summed.at[phase, stream, pl.ds(start, OWN)], from_chips.at[phase, stream, k],
                reduce_send.at[phase, stream, k], reduce_recv.at[phase, stream, k], to_chip[k],
            )

    def reduce_finish(phase, stream):
        total = summed[phase, stream, pl.ds(pl.multiple_of(chip * OWN, OWN), OWN), :]
        for k in range(1, CHIPS):
            arrived(
                from_chips.at[phase, stream, k], reduce_send.at[phase, stream, k],
                reduce_recv.at[phase, stream, k], to_chip[k],
            )
            total += from_chips[phase, stream, k]
        return total

    def gather_start(phase, stream, value):
        mine = pl.ds(pl.multiple_of(chip * OWN, OWN), OWN)
        vectors[phase, stream, core, mine, :] = value
        piece = vectors.at[phase, stream, core, mine]
        for k in range(1, CHIPS):
            send(piece, piece, gather_send.at[phase, stream, k], gather_recv.at[phase, stream, k], to_chip[k])

    def gather_middle(phase, stream):
        for k in range(1, CHIPS):
            start = pl.multiple_of(chip_at(opposite(k)) * OWN, OWN)
            piece = vectors.at[phase, stream, core, pl.ds(start, OWN)]
            arrived(piece, gather_send.at[phase, stream, k], gather_recv.at[phase, stream, k], to_chip[k])
        half = vectors.at[phase, stream, core]
        send(half, half, back_send.at[phase, stream], back_recv.at[phase, stream], to_core)

    def gather_finish(phase, stream):
        half = vectors.at[phase, stream, other_core]
        arrived(half, back_send.at[phase, stream], back_recv.at[phase, stream], to_core)

    def half_rows(half):
        return pl.ds(pl.multiple_of(half * HALF, HALF), HALF)

    for stream in range(STREAMS):
        for half in (other_core, core):
            total = jnp.zeros((HALF, K), F32)
            for slot in range(SLOTS):
                rating = weights[stream, slot, half_rows(half), :]
                weight = jnp.where(rating > 0.0, 1.0 + CONFIDENCE_SCALE * rating, 0.0) * live[slot]
                total += dot3(split(weight), (item_high[slot], item_low[slot]), NN)
            partial[0, stream, half] = total
        reduce_start(0, stream)
    for stream in range(STREAMS):
        reduce_middle(0, stream)
    state = []
    for stream in range(STREAMS):
        rhs = reduce_finish(0, stream)
        gather_start(0, stream, rhs)
        norm = jnp.sum(rhs * rhs, axis=1, keepdims=True)
        state.append((jnp.zeros_like(rhs), rhs, rhs, norm))

    for phase in range(1, ITERS):
        for stream in range(STREAMS):
            gather_middle(phase - 1, stream)
            for order in range(2):
                half = core if order == 0 else other_core
                if order == 1:
                    gather_finish(phase - 1, stream)
                vector = split(vectors[phase - 1, stream, half])
                total = dot3(vector, (gram_high[...], gram_low[...]), NN)
                for slot in range(SLOTS):
                    scores = dot3(vector, (item_high[slot], item_low[slot]), NT)
                    inner = split(weights[stream, slot, half_rows(half), :] * scores)
                    total += dot3(inner, (scaled_high[slot], scaled_low[slot]), NN)
                partial[phase, stream, half] = total
            reduce_start(phase, stream)
        for stream in range(STREAMS):
            reduce_middle(phase, stream)
        for stream in range(STREAMS):
            found, residual, along, norm = state[stream]
            image = reduce_finish(phase, stream) + RIDGE * along
            curvature = jnp.sum(along * image, axis=1, keepdims=True)
            step = norm / (curvature + DIVISOR_GUARD)
            found = found + step * along
            residual = residual - step * image
            norm_next = jnp.sum(residual * residual, axis=1, keepdims=True)
            along = residual + norm_next / (norm + DIVISOR_GUARD) * along
            gather_start(phase, stream, along)
            state[stream] = (found, residual, along, norm_next)

    phase = ITERS - 1
    lane_sums[...] = jnp.zeros_like(lane_sums)
    ones = jnp.ones((8, 128), F32)
    for stream in range(STREAMS):
        gather_middle(phase, stream)
        for order in range(2):
            half = core if order == 0 else other_core
            if order == 1:
                gather_finish(phase, stream)
            rows = vectors[phase, stream, half]
            vector = split(rows)
            squares = rows * dot3(vector, (gram_high[...], gram_low[...]), NN)
            squares = squares[:, :128] + squares[:, 128:]
            for slot in range(SLOTS):
                scores = dot3(vector, (item_high[slot], item_low[slot]), NT)
                weighted = weights[stream, slot, half_rows(half), :] * (scores * scores)
                folded = (weighted[:, :128] + weighted[:, 128:256]) + (weighted[:, 256:384] + weighted[:, 384:])
                squares += (CONFIDENCE_SCALE * live[slot]) * folded
            packed = lax.dot_general(
                ones, squares, NT, precision=lax.Precision.HIGHEST, preferred_element_type=F32
            )
            for piece in range(HALF // 128):
                lane_sums[half, stream, piece, :] = packed[0, piece * 128:(piece + 1) * 128]
    send(lane_sums, lane_core, last_send.at[0], last_recv.at[0], to_core)
    arrived(lane_core, last_send.at[0], last_recv.at[0], to_core)
    lane_total[...] = lane_sums[...] + lane_core[...]
    for k in range(1, CHIPS):
        send(lane_total, lane_chips.at[k], last_send.at[k], last_recv.at[k], to_chip[k])
    total = lane_total[...]
    for k in range(1, CHIPS):
        arrived(lane_chips.at[k], last_send.at[k], last_recv.at[k], to_chip[k])
        total += lane_chips[k]
    owners = 128 // OWN
    for stream in range(STREAMS):
        found, residual, along, norm = state[stream]
        pick = jnp.zeros((8, 128), F32)
        for half in range(2):
            for piece in range(HALF // 128):
                mine = jnp.logical_and(core == half, chip // owners == piece)
                pick = jnp.where(mine, jnp.broadcast_to(total[half, stream, piece][None, :], (8, 128)), pick)
        lanes = lax.broadcasted_iota(jnp.int32, (OWN, 128), 1)
        users = lax.broadcasted_iota(jnp.int32, (OWN, 128), 0)
        pick = jnp.broadcast_to(pick[:1], (OWN, 128))
        curvature = jnp.sum(jnp.where(lanes == (chip % owners) * OWN + users, pick, 0.0), axis=1, keepdims=True)
        curvature = curvature + RIDGE * jnp.sum(along * along, axis=1, keepdims=True)
        out_ref[stream * OWN:(stream + 1) * OWN, :] = found + norm / (curvature + DIVISOR_GUARD) * along

    for copy in pending:
        copy.wait_send()


def per_device(ratings, tile_items, tile_live, item_factors):
    by_owner = ratings.reshape(SLOTS, CHIPS, 2, 16, TB)
    dma = pltpu.SemaphoreType.DMA
    anywhere = pl.BlockSpec(memory_space=pl.ANY)
    scalar = pl.BlockSpec(memory_space=pltpu.SMEM)
    vmem = pltpu.VMEM
    return pl.pallas_call(
        kernel,
        out_shape=jax.ShapeDtypeStruct((16, K), F32),
        in_specs=[scalar, scalar, anywhere, anywhere],
        out_specs=pl.BlockSpec(memory_space=vmem),
        scratch_shapes=[
            vmem((BLOCKS * TB, K), F32),
            vmem((SLOTS, 2, CHIPS, 16, TB), BF16),
            vmem((STREAMS, SLOTS, 2 * HALF, TB), F32),
            vmem((SLOTS, TB, K), BF16),
            vmem((SLOTS, TB, K), BF16),
            vmem((SLOTS, TB, K), BF16),
            vmem((SLOTS, TB, K), BF16),
            vmem((K, K), BF16),
            vmem((K, K), BF16),
            vmem((ITERS, STREAMS, 2, HALF, K), F32),
            vmem((ITERS, STREAMS, 2, HALF, K), F32),
            vmem((ITERS, STREAMS, HALF, K), F32),
            vmem((ITERS, STREAMS, HALF, K), F32),
            vmem((ITERS, STREAMS, CHIPS, OWN, K), F32),
            vmem((STREAMS, OWN, K), F32),
            vmem((2, STREAMS, 8, 128), F32),
            vmem((2, STREAMS, 8, 128), F32),
            vmem((2, STREAMS, 8, 128), F32),
            vmem((CHIPS, 2, STREAMS, 8, 128), F32),
            dma((3,)),
            dma((24,)), dma((24,)),
            dma((10,)), dma((10,)),
            dma((ITERS, STREAMS)), dma((ITERS, STREAMS)),
            dma((ITERS, STREAMS, CHIPS)), dma((ITERS, STREAMS, CHIPS)),
            dma((ITERS, STREAMS, CHIPS)), dma((ITERS, STREAMS, CHIPS)),
            dma((ITERS, STREAMS)), dma((ITERS, STREAMS)),
            dma((CHIPS,)), dma((CHIPS,)),
        ],
        compiler_params=pltpu.CompilerParams(
            collective_id=0, has_side_effects=True, vmem_limit_bytes=48 << 20
        ),
        cost_estimate=pl.CostEstimate(flops=14_000_000_000, bytes_accessed=4_000_000, transcendentals=0),
        name="half_step",
    )(tile_items, tile_live, by_owner, item_factors)


def solution(mesh):
    placed = (
        P("row", "col", None, None),
        P("row", "col"),
        P("row", "col"),
        P(("col", "row"), None),
    )
    return jax.shard_map(
        per_device, mesh=mesh, in_specs=placed, out_specs=P(("row", "col"), None), check_vma=False
    )
```

time: 671 us -> 128 us (0.19)
  waiting for transfers between devices: 473 us -> 0 us
  blocking collectives: 137 us -> 0 us
  Pallas kernels: 0 us -> 124 us
  matrix products: 36.6 us -> 0 us
  between operations: 18.6 us -> 0.01 us
    reduce_scatter x4 -> x0, waiting for transfers between devices: 279 us -> none  [combine(): lax.psum_scatter(partial_rows, 'col', scatter_dimension=0, tiled=True)]
    all_gather x3 -> x0, blocking collectives: 137 us -> none  [per_device(): lax.all_gather(direction, 'col', axis=0, tiled=True)]
    pallas_call x0 -> x1, Pallas kernels: none -> 124 us  [per_device(): pl.pallas_call(kernel, out_shape=jax.ShapeDtypeStruct((16, K), F32), in_s...]
    psum x1 -> x0, waiting for transfers between devices: 123 us -> none  [per_device(): gram_matrix = lax.psum(gram_local, ('row', 'col'))]
    all_gather x1 -> x0, waiting for transfers between devices: 70.8 us -> none  [per_device(): local_items = lax.all_gather(item_factors, 'row', axis=0, tiled=True)]
    dot_general x25 -> x0, matrix products: 36.6 us -> none  [the longest x12 19 us: tile_term(): jnp.dot(inner_part, item_rows, precision=HIGH, preferred_element_type=jnp...]
  transfers between devices with their start and end apart: 6 -> 0, of which waited for: 5 -> 0; matrix products, arithmetic and copies ran while one was open for 2% -> 0% of each run, Pallas kernels for 0% -> 0%
where the time goes in v1:
time: 128 us
  Pallas kernels  124 us (97%)
  local copies, waits for them, and re-layouts  4.23 us (3%)
    pallas_call x1, Pallas kernels, per_device(): pl.pallas_call(kernel, out_shape=jax.ShapeDtypeStruct((16, K), F32), in_s...  124 us
    unnamed x9, local copies, waits for them, and re-layouts  4.23 us

profile of v1, /device:TPU:1, one launch (start us, length us, event | category | flops | bytes accessed | tf_op | source)
XLA Modules:
  0.0 127.8 jit_solution(7930879946046303231)
XLA Ops:
  0.0 0.0 copy-start
  0.0 1.4 %copy-done = bf16[1,3,512,512]{3,2,1,0:T(8,128)(2,1)S(1)} copy-done((bf16[1,3,512,512]{3,2,1,0:T(8,128)(2,1)S(1)}, bf16[1,3,512,512]{3,2,1,0:T(8,128)(2,1)}, u32[]{:S(2)}) %copy-start) | copy-done | bytes 1572888
  1.4 0.0 copy-start.1
  1.4 0.9 copy-done.1
  2.3 0.0 copy-start.2
  2.3 0.7 copy-done.2
  3.0 0.0 copy-start.3
  3.0 0.7 copy-done.3
  3.6 123.5 %half_step.1 = f32[16,256]{1,0:T(8,128)S(1)} custom-call(s32[1,3]{1,0:T(1,128)S(1)} %copy-done.2, s32[1,3]{1,0:T(1,128)S(1)} %copy-done.3, bf16[3,16,2,16,512]{4,3,2,1,0:T(8,128)(2,1)S(1)} %bitcast.1, f32[128,256]{1,0:T(8,128)S(1)} %copy-done.1), custom_call_target="tpu_custom_call" | custom-call | flops 14000000000 | bytes 4000000 | tf_op jit(solution)/shard_map/half_step/pallas_call | solution.py:330
  127.2 0.6 copy.6
Async XLA Ops:
  0.0 1.4 %copy-start = (bf16[1,3,512,512]{3,2,1,0:T(8,128)(2,1)S(1)}, bf16[1,3,512,512]{3,2,1,0:T(8,128)(2,1)}, u32[]{:S(2)}) copy-start(bf16[1,3,512,512]{3,2,1,0:T(8,128)(2,1)} %param.4) | copy-start | bytes 4718596
  1.4 0.9 copy-start.1
  2.3 0.7 copy-start.2
  3.0 0.7 copy-start.3

commit v2 on v1

v2 whole, which is shorter than its diff:
```python
import functools

import jax
import jax.numpy as jnp
from jax import lax
from jax.experimental import pallas as pl
from jax.experimental.pallas import tpu as pltpu
from jax.sharding import PartitionSpec as P

ITERS = 3
CONFIDENCE_SCALE = 40.0
RIDGE = 1.0
DIVISOR_GUARD = 1e-20

K = 256
TB = 512
BLOCKS = 4
SLOTS = 3
Z = 8
CHIPS = 16
STREAMS = 2
OWN = 16 // STREAMS
HALF = CHIPS * OWN
ROWS = 2 * HALF
CUT = 56
SHARE = 128
MESH = pl.DeviceIdType.MESH
F32 = jnp.float32
BF16 = jnp.bfloat16

NN = (((1,), (0,)), ((), ()))
NT = (((1,), (1,)), ((), ()))
TN = (((0,), (0,)), ((), ()))


def split(value):
    high = value.astype(BF16)
    return high, (value - high.astype(F32)).astype(BF16)


def dot(a, b, dims):
    return lax.dot_general(a, b, dims, preferred_element_type=F32)


def dot3(a, b, dims):
    return dot(a[0], b[0], dims) + (dot(a[1], b[0], dims) + dot(a[0], b[1], dims))


def kernel(
    tile_hbm, live_hbm, ratings_ref, items_ref, out_ref,
    tile_ref, live_ref, items, raw, weights, item_high, item_low, scaled_high, scaled_low, gram_high, gram_low,
    gram_even, gram_odd, right,
    vectors, partial, from_core, summed, from_chips, direction, lane_sums, lane_core, lane_total, lane_chips,
    load_sem, z_send, z_recv, y_send, y_recv, core_send, core_recv, reduce_send, reduce_recv,
    gather_send, gather_recv, back_send, back_recv, last_send, last_recv,
):
    row = lax.axis_index("row")
    col = lax.axis_index("col")
    z, y_lo = lax.div(row, 2), lax.rem(row, 2)
    chip, core = lax.div(col, 2), lax.rem(col, 2)
    chip_x, chip_y = lax.div(chip, 4), lax.rem(chip, 4)
    other_core = 1 - core

    ring_x = [chip_x] + [lax.rem(chip_x + step, 4) for step in range(1, 4)]
    ring_y = [chip_y] + [lax.rem(chip_y + step, 4) for step in range(1, 4)]
    chip_at = [ring_x[k // 4] * 4 + ring_y[k % 4] for k in range(CHIPS)]
    owner_rows = [pl.ds(pl.multiple_of(chip_at[k] * OWN, OWN), OWN) for k in range(CHIPS)]
    ring_z = [z] + [lax.rem(z + step, Z) for step in range(1, Z)]

    def opposite(offset):
        return (-(offset // 4) % 4) * 4 + -(offset % 4) % 4

    to_core = (row, chip * 2 + other_core)
    to_y = (z * 2 + 1 - y_lo, col)
    to_z = {1: (ring_z[1] * 2 + y_lo, col), -1: (ring_z[Z - 1] * 2 + y_lo, col)}
    offsets = sorted(
        range(1, CHIPS), key=lambda k: min(k // 4, 4 - k // 4) + 2 * min(k % 4, 4 - k % 4), reverse=True
    )
    to_chip = {k: (row, chip_at[k] * 2 + core) for k in range(1, CHIPS)}

    pending = []

    def send(src, dst, send_sem, recv_sem, device):
        copy = pltpu.make_async_remote_copy(
            src_ref=src, dst_ref=dst, send_sem=send_sem, recv_sem=recv_sem, device_id=device, device_id_type=MESH
        )
        copy.start()
        pending.append(copy)

    def arrived(dst, send_sem, recv_sem, device):
        pltpu.make_async_remote_copy(
            src_ref=dst, dst_ref=dst, send_sem=send_sem, recv_sem=recv_sem, device_id=device, device_id_type=MESH
        ).wait_recv()

    share_start = {
        (step, side): (ring_z[step] * 2 + (1 - y_lo if side else y_lo)) * SHARE for step in range(Z) for side in (0, 1)
    }

    def item_rows(step, side, first, count):
        return items.at[pl.ds(pl.multiple_of(share_start[step, side] + first, 8), count)]

    own_load = pltpu.make_async_copy(items_ref, item_rows(0, 0, 0, SHARE), load_sem.at[0])
    own_load.start()
    rating_loads = [
        pltpu.make_async_copy(ratings_ref.at[:, :, c], raw.at[:, c], load_sem.at[1 + c]) for c in range(2)
    ]
    scalar_loads = [
        pltpu.make_async_copy(tile_hbm, tile_ref, load_sem.at[3]),
        pltpu.make_async_copy(live_hbm, live_ref, load_sem.at[4]),
    ]
    for load in scalar_loads + rating_loads:
        load.start()

    barrier = pltpu.get_barrier_semaphore()
    neighbours = [to_core, to_y, to_z[1], to_z[-1]] + list(to_chip.values())
    for device in neighbours:
        pl.semaphore_signal(barrier, inc=1, device_id=device, device_id_type=MESH)
    own_load.wait()
    pl.semaphore_wait(barrier, len(neighbours))

    def chunk_tasks(step):
        z_of = ring_z[step]
        block_of = lax.div(z_of, 2)
        chunk = pl.ds(pl.multiple_of(z_of * (2 * SHARE), 2 * SHARE), 2 * SHARE)
        columns = pl.ds(pl.multiple_of(lax.rem(z_of, 2) * (2 * SHARE), 2 * SHARE), 2 * SHARE)

        def gram_terms():
            high, low = split(items[chunk, :])
            gram_even[...] += dot(high, high, TN)
            gram_odd[...] += dot(high, low, TN)

        def right_terms(stream, first):
            users = pl.ds(first, 256)
            scales = [
                (tile_ref[0, slot] == block_of).astype(F32) * live_ref[0, slot].astype(F32) for slot in range(SLOTS)
            ]
            rating = weights[stream, 0, users, columns] * scales[0]
            for slot in range(1, SLOTS):
                rating += weights[stream, slot, users, columns] * scales[slot]
            weight = jnp.where(rating > 0.0, 1.0 + CONFIDENCE_SCALE * rating, 0.0)
            right[stream, users, :] += dot3(split(weight), split(items[chunk, :]), NN)

        tasks.append(gram_terms)
        for stream in range(STREAMS):
            for first in range(0, ROWS, 256):
                tasks.append(functools.partial(right_terms, stream, first))

    tasks = []

    pieces = [(1, CUT, 40), (1, CUT + 40, SHARE - CUT - 40)]
    pieces += [(0, 0, 32), (0, 32, CUT - 32), (2, 0, 32), (2, 32, CUT - 32)]
    reach = {(0, 1): 4, (0, -1): 3, (1, 1): 3, (1, -1): 4, (2, 1): 4, (2, -1): 3}

    def z_source(way, hop):
        return -way * hop % Z

    def z_piece(number, way, hop):
        kind, first, count = pieces[number]
        return item_rows(z_source(way, hop), kind // 2, first, count)

    def z_index(number, way, hop):
        return (number * 2 + (way + 1) // 2) * 4 + hop - 1

    crossings = {}
    crossing_count = []

    def cross(key, step, first, count):
        index = len(crossing_count)
        crossing_count.append(index)
        crossings.setdefault(key, []).append((index, step, first, count))
        piece = item_rows(step, 0, first, count)
        send(piece, piece, y_send.at[index], y_recv.at[index], to_y)

    def crossed(key):
        for index, step, first, count in crossings.pop(key):
            arrived(item_rows(step, 1, first, count), y_send.at[index], y_recv.at[index], to_y)

    for kind, first, count in pieces:
        if kind == 0:
            cross(("first", first), 0, first, count)
    for hop in range(1, 6):
        for number, (kind, first, count) in enumerate(pieces):
            for way in (1, -1):
                index = z_index(number, way, hop - 1)
                if 1 < hop <= reach[kind, way] + 1:
                    arrived(z_piece(number, way, hop - 1), z_send.at[index], z_recv.at[index], to_z[-way])
                elif hop == 1 and kind == 2 and way == 1:
                    crossed(("first", first))
                if hop <= reach[kind, way]:
                    piece = z_piece(number, way, hop - 1)
                    index = z_index(number, way, hop)
                    send(piece, piece, z_send.at[index], z_recv.at[index], to_z[way])
                if kind == 1 and (way == 1 if hop == 1 else hop <= reach[kind, way] + 1):
                    cross(("rest", hop - 1, way), z_source(way, hop - 1), first, count)
                if tasks and hop > 2:
                    tasks.pop(0)()
        if hop == 1:
            for load in scalar_loads + rating_loads:
                load.wait()
            for slot in range(SLOTS):
                for half in range(2):
                    block = raw[slot, half].astype(F32)
                    for stream in range(STREAMS):
                        part = block[:, stream * OWN:(stream + 1) * OWN, :]
                        weights[stream, slot, half * HALF:(half + 1) * HALF, :] = part.reshape(HALF, TB)
            gram_even[...] = jnp.zeros_like(gram_even)
            gram_odd[...] = jnp.zeros_like(gram_odd)
            right[...] = jnp.zeros_like(right)
        elif hop == 2:
            crossed(("rest", 0, 1))
            chunk_tasks(0)
        else:
            for way in (1, -1):
                crossed(("rest", hop - 2, way))
                chunk_tasks(z_source(way, hop - 2))
    while tasks:
        tasks.pop(0)()
    crossed(("rest", 4, -1))
    chunk_tasks(z_source(1, 4))
    while tasks:
        tasks.pop(0)()

    live = [live_ref[0, slot].astype(F32) for slot in range(SLOTS)]

    def pick_items(slot):
        block = jnp.zeros((TB, K), F32)
        for index in range(BLOCKS):
            block += (tile_ref[0, slot] == index).astype(F32) * items[index * TB:(index + 1) * TB, :]
        item_high[slot], item_low[slot] = split(block)
        scaled_high[slot], scaled_low[slot] = split(block * (CONFIDENCE_SCALE * live[slot]))

    def reduce_start(phase, stream):
        send(
            partial.at[phase, stream, other_core], from_core.at[phase, stream],
            core_send.at[phase, stream], core_recv.at[phase, stream], to_core,
        )

    def reduce_middle(phase, stream):
        arrived(from_core.at[phase, stream], core_send.at[phase, stream], core_recv.at[phase, stream], to_core)
        summed[phase, stream] = partial[phase, stream, core] + from_core[phase, stream]
        for k in offsets:
            send(
                summed.at[phase, stream, owner_rows[k]], from_chips.at[phase, stream, k],
                reduce_send.at[phase, stream, k], reduce_recv.at[phase, stream, k], to_chip[k],
            )

    def reduce_finish(phase, stream):
        total = summed[phase, stream, owner_rows[0], :]
        for k in range(1, CHIPS):
            arrived(
                from_chips.at[phase, stream, k], reduce_send.at[phase, stream, k],
                reduce_recv.at[phase, stream, k], to_chip[k],
            )
            total += from_chips[phase, stream, k]
        return total

    def gather_start(phase, stream, value):
        mine = owner_rows[0]
        vectors[phase, stream, core, mine, :] = value
        piece = vectors.at[phase, stream, core, mine]
        for k in offsets:
            send(piece, piece, gather_send.at[phase, stream, k], gather_recv.at[phase, stream, k], to_chip[k])

    def gather_middle(phase, stream):
        for k in range(1, CHIPS):
            piece = vectors.at[phase, stream, core, owner_rows[opposite(k)]]
            arrived(piece, gather_send.at[phase, stream, k], gather_recv.at[phase, stream, k], to_chip[k])
        half = vectors.at[phase, stream, core]
        send(half, half, back_send.at[phase, stream], back_recv.at[phase, stream], to_core)

    def gather_finish(phase, stream):
        half = vectors.at[phase, stream, other_core]
        arrived(half, back_send.at[phase, stream], back_recv.at[phase, stream], to_core)

    for stream in range(STREAMS):
        partial[0, stream] = right[stream].reshape(2, HALF, K)
        reduce_start(0, stream)
    pick_items(0)
    for stream in range(STREAMS):
        reduce_middle(0, stream)
    for slot in range(1, SLOTS):
        pick_items(slot)
    gram_high[...], gram_low[...] = split(gram_even[...] + (gram_odd[...] + gram_odd[...].T))
    state = []
    for stream in range(STREAMS):
        rhs = reduce_finish(0, stream)
        gather_start(0, stream, rhs)
        norm = jnp.sum(rhs * rhs, axis=1, keepdims=True)
        state.append((jnp.zeros_like(rhs), rhs, rhs, norm))

    for phase in range(1, ITERS):
        for stream in range(STREAMS):
            gather_middle(phase - 1, stream)
            if stream:
                reduce_middle(phase, stream - 1)
            gather_finish(phase - 1, stream)
            vector = split(vectors[phase - 1, stream].reshape(ROWS, K))
            total = dot3(vector, (gram_high[...], gram_low[...]), NN)
            for slot in range(SLOTS):
                scores = dot3(vector, (item_high[slot], item_low[slot]), NT)
                inner = split(weights[stream, slot] * scores)
                total += dot3(inner, (scaled_high[slot], scaled_low[slot]), NN)
            partial[phase, stream] = total.reshape(2, HALF, K)
            reduce_start(phase, stream)
        reduce_middle(phase, STREAMS - 1)
        for stream in range(STREAMS):
            found, residual, along, norm = state[stream]
            image = reduce_finish(phase, stream) + RIDGE * along
            curvature = jnp.sum(along * image, axis=1, keepdims=True)
            step = norm / (curvature + DIVISOR_GUARD)
            found = found + step * along
            residual = residual - step * image
            norm_next = jnp.sum(residual * residual, axis=1, keepdims=True)
            along = residual + norm_next / (norm + DIVISOR_GUARD) * along
            gather_start(phase, stream, along)
            state[stream] = (found, residual, along, norm_next)

    phase = ITERS - 1
    lane_sums[...] = jnp.zeros_like(lane_sums)
    ones = jnp.ones((8, 128), F32)

    def lane_row(half, stream, piece):
        return (half * STREAMS + stream) * (HALF // 128) + piece

    for stream in range(STREAMS):
        gather_middle(phase, stream)
        gather_finish(phase, stream)
        rows = vectors[phase, stream].reshape(ROWS, K)
        vector = split(rows)
        squares = rows * dot3(vector, (gram_high[...], gram_low[...]), NN)
        squares = squares[:, :128] + squares[:, 128:]
        for slot in range(SLOTS):
            scores = dot3(vector, (item_high[slot], item_low[slot]), NT)
            weighted = weights[stream, slot] * (scores * scores)
            folded = (weighted[:, :128] + weighted[:, 128:256]) + (weighted[:, 256:384] + weighted[:, 384:])
            squares += (CONFIDENCE_SCALE * live[slot]) * folded
        packed = lax.dot_general(
            ones, squares, NT, precision=lax.Precision.HIGHEST, preferred_element_type=F32
        )
        for half in range(2):
            for piece in range(HALF // 128):
                start = half * HALF + piece * 128
                lane_sums[lane_row(half, stream, piece), :] = packed[0, start:start + 128]
    send(lane_sums, lane_core, last_send.at[0], last_recv.at[0], to_core)
    arrived(lane_core, last_send.at[0], last_recv.at[0], to_core)
    lane_total[...] = lane_sums[...] + lane_core[...]
    for k in offsets:
        send(lane_total, lane_chips.at[k], last_send.at[k], last_recv.at[k], to_chip[k])
    total = lane_total[...]
    for k in range(1, CHIPS):
        arrived(lane_chips.at[k], last_send.at[k], last_recv.at[k], to_chip[k])
        total += lane_chips[k]
    owners = 128 // OWN
    for stream in range(STREAMS):
        found, residual, along, norm = state[stream]
        pick = jnp.zeros((8, 128), F32)
        for half in range(2):
            for piece in range(HALF // 128):
                mine = jnp.logical_and(core == half, lax.div(chip, owners) == piece)
                pick = jnp.where(mine, jnp.broadcast_to(total[lane_row(half, stream, piece)][None, :], (8, 128)), pick)
        lanes = lax.broadcasted_iota(jnp.int32, (OWN, 128), 1)
        users = lax.broadcasted_iota(jnp.int32, (OWN, 128), 0)
        pick = jnp.broadcast_to(pick[:1], (OWN, 128))
        curvature = jnp.sum(jnp.where(lanes == lax.rem(chip, owners) * OWN + users, pick, 0.0), axis=1, keepdims=True)
        curvature = curvature + RIDGE * jnp.sum(along * along, axis=1, keepdims=True)
        out_ref[stream * OWN:(stream + 1) * OWN, :] = found + norm / (curvature + DIVISOR_GUARD) * along

    for copy in pending:
        copy.wait_send()


def per_device(ratings, tile_items, tile_live, item_factors):
    by_owner = ratings.reshape(SLOTS, CHIPS, 2, 16, TB)
    dma = pltpu.SemaphoreType.DMA
    in_hbm = pl.BlockSpec(memory_space=pltpu.HBM)
    vmem = pltpu.VMEM
    return pl.pallas_call(
        kernel,
        out_shape=jax.ShapeDtypeStruct((16, K), F32),
        in_specs=[in_hbm] * 4,
        out_specs=pl.BlockSpec(memory_space=vmem),
        scratch_shapes=[
            pltpu.SMEM((1, SLOTS), jnp.int32),
            pltpu.SMEM((1, SLOTS), jnp.int32),
            vmem((BLOCKS * TB, K), F32),
            vmem((SLOTS, 2, CHIPS, 16, TB), BF16),
            vmem((STREAMS, SLOTS, ROWS, TB), F32),
            vmem((SLOTS, TB, K), BF16),
            vmem((SLOTS, TB, K), BF16),
            vmem((SLOTS, TB, K), BF16),
            vmem((SLOTS, TB, K), BF16),
            vmem((K, K), BF16),
            vmem((K, K), BF16),
            vmem((K, K), F32),
            vmem((K, K), F32),
            vmem((STREAMS, ROWS, K), F32),
            vmem((ITERS, STREAMS, 2, HALF, K), F32),
            vmem((ITERS, STREAMS, 2, HALF, K), F32),
            vmem((ITERS, STREAMS, HALF, K), F32),
            vmem((ITERS, STREAMS, HALF, K), F32),
            vmem((ITERS, STREAMS, CHIPS, OWN, K), F32),
            vmem((STREAMS, OWN, K), F32),
            vmem((8, 128), F32),
            vmem((8, 128), F32),
            vmem((8, 128), F32),
            vmem((CHIPS, 8, 128), F32),
            dma((5,)),
            dma((48,)), dma((48,)),
            dma((18,)), dma((18,)),
            dma((ITERS, STREAMS)), dma((ITERS, STREAMS)),
            dma((ITERS, STREAMS, CHIPS)), dma((ITERS, STREAMS, CHIPS)),
            dma((ITERS, STREAMS, CHIPS)), dma((ITERS, STREAMS, CHIPS)),
            dma((ITERS, STREAMS)), dma((ITERS, STREAMS)),
            dma((CHIPS,)), dma((CHIPS,)),
        ],
        compiler_params=pltpu.CompilerParams(
            collective_id=0, has_side_effects=True, vmem_limit_bytes=63 << 20
        ),
        cost_estimate=pl.CostEstimate(flops=14_000_000_000, bytes_accessed=4_000_000, transcendentals=0),
        name="half_step",
    )(tile_items, tile_live, by_owner, item_factors)


def solution(mesh):
    placed = (
        P("row", "col", None, None),
        P("row", "col"),
        P("row", "col"),
        P(("col", "row"), None),
    )
    return jax.shard_map(
        per_device, mesh=mesh, in_specs=placed, out_specs=P(("row", "col"), None), check_vma=False
    )
```

time: 128 us -> 105 us (0.82)
  Pallas kernels: 124 us -> 102 us
  local copies, waits for them, and re-layouts: 4.23 us -> 1.32 us
    pallas_call x1, Pallas kernels: 124 us -> 102 us  [per_device(): pl.pallas_call(kernel, out_shape=jax.ShapeDtypeStruct((16, K), F32), in_s...]
    unnamed x9 -> x1, local copies, waits for them, and re-layouts: 4.23 us -> 1.32 us
where the time goes in v2:
time: 105 us; the launch traced here: 104 us
  Pallas kernels  102 us (97%)
  local copies, waits for them, and re-layouts  1.32 us (1%)
    pallas_call x1, Pallas kernels, per_device(): pl.pallas_call(kernel, out_shape=jax.ShapeDtypeStruct((16, K), F32), in_s...  102 us

profile of v2, /device:TPU:1, one launch (start us, length us, event | category | flops | bytes accessed | tf_op | source)
XLA Modules:
  0.0 103.8 jit_solution(6561245594960141007)
XLA Ops:
  0.0 102.5 %half_step.1 = f32[16,256]{1,0:T(8,128)} custom-call(s32[1,3]{1,0:T(1,128)} %tile_hbm.1, s32[1,3]{1,0:T(1,128)} %live_hbm.1, bf16[3,16,2,16,512]{4,3,2,1,0:T(8,128)(2,1)} %bitcast.1, f32[128,256]{1,0:T(8,128)} %items_ref.1), custom_call_target="tpu_custom_call" | custom-call | flops 14000000000 | bytes 4000000 | tf_op jit(solution)/shard_map/half_step/pallas_call | solution.py:377
  102.5 1.3 %copy.6 = f32[16,256]{1,0:T(8,128)} copy(f32[16,256]{1,0:T(8,128)} %half_step.1) | data formatting | bytes 32768
